TPU v7x, 256 devices: a whole 4x4x8 slice. The times are simulated.
256 devices in a mesh: freq: 64 (over z, y, core), col: 4 (over x).
Axes of the slice: x: 4, y: 4, z: 8, core: 2. Of those that a mesh axis runs over, the one named last changes fastest.
Arguments:
- traces: bfloat16 [16, 512, 64, 512], P('col', 'freq'), may hold values from -6 to 6
- left_factors: bfloat16 [256, 16, 16, 16, 512], P('freq', None, 'col'), may hold values from -0.5 to 0.5
- right_factors: bfloat16 [256, 16, 16, 16, 512], P('freq', None, 'col'), may hold values from -0.25 to 0.25
- tile_ranks: int32 [256, 16, 16], P('freq', None, 'col'), may hold values from 1 to 16, as said below
Outputs:
- modelled: bfloat16 [16, 512, 64, 512], P('col', 'freq')
Inputs may be any that keep to these rules, and one draw needn't show every extreme that they name: `tile_ranks`: the rank of each kernel tile; factor rows at or past it are not part of the kernel. 16 is reached by some tile in every draw.
All inputs are finite; a program needn't handle non-finite values.
Results may differ from a plain program's by a relative error of at most 0.0072.
Values may be sent and summed in bfloat16 or wider, within the bound.
A program may use at most 128 MiB of HBM per device.

v0:
```python
import jax
import jax.numpy as jnp
from jax import lax
from jax.sharding import PartitionSpec as P


def split_up(shard, dim, size):
    before, after = (shard.shape[:dim], shard.shape[dim + 1 :])
    return jnp.moveaxis(shard.reshape(*before, size, -1, *after), dim, 0)


def cut_rows(length, count):
    step = length // count
    if step >= 8:
        step -= step % 8
    return [step * k for k in range(1, count)]


def laid_out(parts, dim):
    lengths = list(parts.shape[1:])
    lengths[dim] *= parts.shape[0]
    return jnp.moveaxis(parts, 0, dim).reshape(lengths)


def cut_exchange(shard, axis, pieces, split_dim, concat_dim):
    parts = split_up(shard, split_dim, lax.axis_size(axis))
    cut = max(range(1, max(2, parts.ndim - 1)), key=lambda d: parts.shape[d])
    gathered = []
    for piece in jnp.split(parts, cut_rows(parts.shape[cut], pieces), axis=cut):
        if piece.size:
            gathered.append(lax.all_to_all(piece, axis, split_axis=0, concat_axis=0, tiled=True))
    return laid_out(jnp.concatenate(gathered, axis=cut), concat_dim)


def hartley_table(time_count, freq_count):
    times = jnp.arange(time_count, dtype=jnp.int32)
    freqs = jnp.arange(freq_count, dtype=jnp.int32)
    phase = times[:, None] * freqs[None, :] % time_count
    angle = 2.0 * jnp.pi / time_count * phase.astype(jnp.float32)
    scale = jnp.sqrt(jnp.float32(time_count))
    return ((jnp.cos(angle) + jnp.sin(angle)) / scale).astype(jnp.bfloat16)


def tile_coeffs(spectrum, right_tiles, rank_tiles):
    coeffs = jnp.einsum("cws,rcks->rwck", spectrum, right_tiles, preferred_element_type=jnp.float32)
    kept_mask = (
        lax.broadcasted_iota(jnp.int32, (1, 1, 1, right_tiles.shape[2]), 3)
        < rank_tiles[:, None, :, None]
    )
    return jnp.where(kept_mask, coeffs, 0.0).astype(jnp.bfloat16)


def shards(traces, left_factors, right_factors, tile_ranks):
    freq_local = left_factors.shape[0]
    cas_table = hartley_table(traces.shape[3], freq_local * lax.axis_size("freq"))
    left_rows = cut_exchange(left_factors, "col", 2, 1, 2)
    spectra_local = jnp.einsum(
        "cswt,tk->kcws", traces, cas_table, preferred_element_type=jnp.float32
    ).astype(jnp.bfloat16)

    def frequency_coeffs(spectrum, right_tiles, rank_tiles):
        return tile_coeffs(spectrum, right_tiles, rank_tiles)

    spec_items = lax.all_to_all(spectra_local, "freq", split_axis=0, concat_axis=3, tiled=True)
    exchanged = jnp.stack(
        [
            frequency_coeffs(spec_items[index], right_factors[index], tile_ranks[index])
            for index in range(freq_local)
        ]
    )
    coeff_rows = lax.all_to_all(exchanged, "col", split_axis=1, concat_axis=3, tiled=True)
    synthesis = jnp.einsum(
        "frwck,frcks->frws", coeff_rows, left_rows, preferred_element_type=jnp.float32
    ).astype(jnp.bfloat16)
    return jnp.einsum(
        "krws,tk->rswt",
        lax.all_to_all(synthesis, "freq", split_axis=3, concat_axis=0, tiled=True),
        cas_table,
        preferred_element_type=jnp.float32,
    ).astype(jnp.bfloat16)


def solution(mesh):
    in_specs = (
        P("col", "freq", None, None),
        P("freq", None, "col", None, None),
        P("freq", None, "col", None, None),
        P("freq", None, "col"),
    )
    out_specs = P("col", "freq", None, None)
    return jax.shard_map(shards, mesh=mesh, in_specs=in_specs, out_specs=out_specs, check_vma=False)
```

profile of v0, /device:TPU:1, one launch (start us, length us, event | category | flops | bytes accessed | tf_op | source)
XLA Modules:
  0.0 181.9 jit_solution(851206235879893282)
XLA Ops:
  0.0 4.2 %fusion.50 = (bf16[4,4,4,4,8,512]{5,4,3,2,0,1:T(8,128)(2,1)S(1)}, bf16[4,4,4,4,8,512]{5,4,3,2,0,1:T(8,128)(2,1)}) fusion(bf16[4,4,4,4,16,512]{5,4,3,2,0,1:T(8,128)(2,1)} %bitcast.136), kind=kLoop, calls=%fused_computation.72 | loop fusion | bytes 8388608 | tf_op jit(solution)/shard_map/split | solution.py:29
  5.6 4.8 %all-to-all-start.2 = ((bf16[4,4,4,4,8,512]{5,4,3,2,1,0:T(8,128)(2,1)}), bf16[4,4,4,4,8,512]{5,4,3,2,1,0:T(8,128)(2,1)}, u32[]{:S(2)}, u32[]{:S(2)}) async-start(bf16[4,4,4,4,8,512]{5,4,3,2,1,0:T(8,128)(2,1)} %copy.69), calls=%async_computation.2 | async-start | bytes 4194304 | tf_op jit(solution)/shard_map/all_to_all | solution.py:31
  10.4 3.5 %fusion.4 = bf16[256,4,64,8]{0,2,3,1:T(8,128)(2,1)S(1)} fusion(bf16[4,8,64,512]{3,2,1,0:T(8,128)(2,1)S(1)} %copy-done), kind=kOutput, calls=%fused_computation.7 | convolution fusion | flops 539623424 | bytes 3145728 | tf_op jit(solution)/shard_map/cswt,tk->kcws/dot_general | solution.py:57
  13.9 3.8 %copy.54 = bf16[256,4,64,8]{2,3,1,0:T(8,128)(2,1)} copy(bf16[256,4,64,8]{0,2,3,1:T(8,128)(2,1)S(1)} %fusion.4) | data formatting | bytes 2097152 | tf_op jit(solution)/shard_map/convert_element_type | solution.py:59
  17.7 4.7 %reshape.52 = bf16[64,2,4096]{2,1,0:T(2,128)(2,1)} reshape(bf16[256,4,8,64]{3,2,1,0:T(8,128)(2,1)} %bitcast.131) | data formatting | bytes 2097152
  22.4 12.1 %all-to-all-done.2 = bf16[4,4,4,4,8,512]{5,4,3,2,1,0:T(8,128)(2,1)} async-done(((bf16[4,4,4,4,8,512]{5,4,3,2,1,0:T(8,128)(2,1)}), bf16[4,4,4,4,8,512]{5,4,3,2,1,0:T(8,128)(2,1)}, u32[]{:S(2)}, u32[]{:S(2)}) %all-to-all-start.2) | async-done | bytes 2097184 | tf_op jit(solution)/shard_map/all_to_all | solution.py:31
  34.5 15.5 %all-to-all-start = ((bf16[64,2,4096]{2,1,0:T(2,128)(2,1)}), bf16[64,2,4096]{2,1,0:T(2,128)(2,1)S(1)}, u32[]{:S(2)}, u32[]{:S(2)}) async-start(bf16[64,2,4096]{2,1,0:T(2,128)(2,1)} %reshape.52), calls=%async_computation | async-start | bytes 2097152 | tf_op jit(solution)/shard_map/all_to_all | solution.py:64
  50.0 3.3 %copy.70 = bf16[4,4,4,4,8,512]{5,4,3,2,1,0:T(8,128)(2,1)} copy(bf16[4,4,4,4,8,512]{5,4,3,2,0,1:T(8,128)(2,1)} %get-tuple-element.6) | data formatting | bytes 4194304 | tf_op jit(solution)/shard_map/split | solution.py:29
  53.4 2.4 %fusion.51 = (bf16[1,16,4,16,512]{4,3,2,1,0:T(8,128)(2,1)}, bf16[1,16,4,16,512]{4,3,2,1,0:T(8,128)(2,1)}, bf16[1,16,4,16,512]{4,3,2,1,0:T(8,128)(2,1)}, bf16[1,16,4,16,512]{4,3,2,1,0:T(8,128)(2,1)}) fusion(bf16[4,16,4,16,512]{4,3,2,1,0:T(8,128)(2,1)S(1)} %copy-done.1), kind=kLoop, calls=%fused_computation.73 | loop fusion | bytes 8388608 | tf_op jit(solution)/shard_map/slice | solution.py:67
  55.8 22.2 %all-to-all-done = bf16[64,2,4096]{2,1,0:T(2,128)(2,1)S(1)} async-done(((bf16[64,2,4096]{2,1,0:T(2,128)(2,1)}), bf16[64,2,4096]{2,1,0:T(2,128)(2,1)S(1)}, u32[]{:S(2)}, u32[]{:S(2)}) %all-to-all-start) | async-done | bytes 1048608 | tf_op jit(solution)/shard_map/all_to_all | solution.py:64
  78.0 4.5 %all-to-all-start.3 = ((bf16[4,4,4,4,8,512]{5,4,3,2,1,0:T(8,128)(2,1)}), bf16[4,4,4,4,8,512]{5,4,3,2,1,0:T(8,128)(2,1)}, u32[]{:S(2)}, u32[]{:S(2)}) async-start(bf16[4,4,4,4,8,512]{5,4,3,2,1,0:T(8,128)(2,1)} %copy.70), calls=%async_computation.3 | async-start | bytes 4194304 | tf_op jit(solution)/shard_map/all_to_all | solution.py:31
  82.6 2.3 %reshape.53 = bf16[256,4,8,64]{3,2,1,0:T(8,128)(2,1)} reshape(bf16[64,2,4096]{2,1,0:T(2,128)(2,1)S(1)} %all-to-all-done) | data formatting | bytes 2097152
  84.9 2.0 %fusion.52 = (bf16[1,4,64,64,8]{2,4,1,0,3:T(8,128)(2,1)S(1)}, bf16[1,4,64,64,8]{2,4,1,0,3:T(8,128)(2,1)S(1)}, bf16[1,4,64,64,8]{2,4,1,0,3:T(8,128)(2,1)S(1)}, bf16[1,4,64,64,8]{2,4,1,0,3:T(8,128)(2,1)S(1)}) fusion(bf16[4,4,64,64,8]{2,4,1,0,3:T(8,128)(2,1)} %bitcast.133), kind=kLoop, calls=%fused_computation.74 | loop fusion | bytes 2097152 | tf_op jit(solution)/shard_map/slice | solution.py:67
  92.2 15.3 %all-to-all-done.3 = bf16[4,4,4,4,8,512]{5,4,3,2,1,0:T(8,128)(2,1)} async-done(((bf16[4,4,4,4,8,512]{5,4,3,2,1,0:T(8,128)(2,1)}), bf16[4,4,4,4,8,512]{5,4,3,2,1,0:T(8,128)(2,1)}, u32[]{:S(2)}, u32[]{:S(2)}) %all-to-all-start.3) | async-done | bytes 2097184 | tf_op jit(solution)/shard_map/all_to_all | solution.py:31
  107.5 4.3 %all-to-all-start.1 = ((bf16[4,2,32768]{2,1,0:T(2,128)(2,1)}), bf16[4,2,32768]{2,1,0:T(2,128)(2,1)}, u32[]{:S(2)}, u32[]{:S(2)}) async-start(bf16[4,2,32768]{2,1,0:T(2,128)(2,1)} %reshape.54), calls=%async_computation.1 | async-start | bytes 1048576 | tf_op jit(solution)/shard_map/all_to_all | solution.py:71
  111.9 2.8 %maximum_bitcast_fusion = bf16[4,4,4,4,16,512]{5,4,3,1,0,2:T(8,128)(2,1)S(1)} fusion(bf16[4,4,4,4,8,512]{5,4,3,2,1,0:T(8,128)(2,1)} %all-to-all-done.3, bf16[4,4,4,4,8,512]{5,4,3,2,1,0:T(8,128)(2,1)} %all-to-all-done.2), kind=kLoop, calls=%fused_computation | loop fusion | flops 8388608 | bytes 8388608 | tf_op jit(solution)/shard_map/transpose | solution.py:22
  114.6 2.5 %copy.71 = bf16[4,4,4,4,16,512]{5,4,3,2,1,0:T(8,128)(2,1)} copy(bf16[4,4,4,4,16,512]{5,4,3,1,0,2:T(8,128)(2,1)S(1)} %maximum_bitcast_fusion) | data formatting | bytes 8388608 | tf_op jit(solution)/shard_map/transpose | solution.py:22
  120.7 3.0 %bitcast_convert_fusion = bf16[4,4,64,512]{3,2,1,0:T(8,128)(2,1)S(1)} fusion(bf16[4,4,64,16,16]{2,4,3,1,0:T(8,128)(2,1)S(1)} %bitcast.138, bf16[4,4,16,16,512]{4,3,2,1,0:T(8,128)(2,1)} %bitcast.130), kind=kOutput, calls=%fused_computation.1 | convolution fusion | flops 268959744 | bytes 5767168 | tf_op jit(solution)/shard_map/frwck,frcks->frws/dot_general | solution.py:72
  123.7 2.9 %copy.72 = bf16[4,4,64,512]{2,1,0,3:T(4,128)(2,1)} copy(bf16[4,4,64,512]{3,2,1,0:T(8,128)(2,1)S(1)} %bitcast_convert_fusion) | data formatting | bytes 2097152 | tf_op jit(solution)/shard_map/convert_element_type | solution.py:74
  126.6 4.4 %reshape.56 = bf16[64,2,4096]{2,1,0:T(2,128)(2,1)S(1)} reshape(bf16[512,4,4,64]{3,2,1,0:T(4,128)(2,1)} %bitcast.132) | data formatting | bytes 2097152
  131.0 38.1 %all_to_all.61 = bf16[64,2,4096]{2,1,0:T(2,128)(2,1)} all-to-all(bf16[64,2,4096]{2,1,0:T(2,128)(2,1)S(1)} %reshape.56), channel_id=1, replica_groups=mesh['freq'=64,'col'=4] {'freq'}, dimensions={0} | all-to-all | bytes 2097152 | tf_op jit(solution)/shard_map/all_to_all | solution.py:77
  169.1 5.3 %reshape.57 = bf16[512,4,4,64]{3,2,1,0:T(4,128)(2,1)} reshape(bf16[64,2,4096]{2,1,0:T(2,128)(2,1)} %all_to_all.61) | data formatting | bytes 2097152
  174.4 2.1 %copy.124 = bf16[4,4,64,512]{2,3,1,0:T(8,128)(2,1)S(1)} copy(bf16[4,4,64,512]{2,1,0,3:T(4,128)(2,1)} %bitcast.134) | data formatting | bytes 2097152 | tf_op jit(solution)/shard_map/all_to_all | solution.py:77
  177.1 4.8 %convert_bitcast_fusion = bf16[4,8,64,512]{3,2,1,0:T(8,128)(2,1)} fusion(bf16[256,4,64,8]{2,3,1,0:T(8,128)(2,1)S(1)} %bitcast.139), kind=kOutput, calls=%fused_computation.5 | convolution fusion | flops 540147712 | bytes 3145728 | tf_op jit(solution)/shard_map/krws,tk->rswt/dot_general | solution.py:75
  (28 shorter events, 10.9 us)
Async XLA Ops:
  0.0 10.4 %copy-start = (bf16[4,8,64,512]{3,2,1,0:T(8,128)(2,1)S(1)}, bf16[4,8,64,512]{3,2,1,0:T(8,128)(2,1)}, u32[]{:S(2)}) copy-start(bf16[4,8,64,512]{3,2,1,0:T(8,128)(2,1)} %param.4) | copy-start | bytes 6291460
  5.6 28.9 %all-to-all-start.2 = ((bf16[4,4,4,4,8,512]{5,4,3,2,1,0:T(8,128)(2,1)}), bf16[4,4,4,4,8,512]{5,4,3,2,1,0:T(8,128)(2,1)}, u32[]{:S(2)}, u32[]{:S(2)}) async-start(bf16[4,4,4,4,8,512]{5,4,3,2,1,0:T(8,128)(2,1)} %copy.69), calls=%async_computation.2 | async-start | bytes 4194304 | tf_op jit(solution)/shard_map/all_to_all | solution.py:31
  34.5 18.8 %copy-start.6 = (s32[4,16,4]{1,2,0:T(4,128)S(1)}, s32[4,16,4]{1,2,0:T(4,128)}, u32[]{:S(2)}) copy-start(s32[4,16,4]{1,2,0:T(4,128)} %param.7) | copy-start | bytes 3076
  34.5 43.5 %all-to-all-start = ((bf16[64,2,4096]{2,1,0:T(2,128)(2,1)}), bf16[64,2,4096]{2,1,0:T(2,128)(2,1)S(1)}, u32[]{:S(2)}, u32[]{:S(2)}) async-start(bf16[64,2,4096]{2,1,0:T(2,128)(2,1)} %reshape.52), calls=%async_computation | async-start | bytes 2097152 | tf_op jit(solution)/shard_map/all_to_all | solution.py:64
  50.0 3.4 %copy-start.1 = (bf16[4,16,4,16,512]{4,3,2,1,0:T(8,128)(2,1)S(1)}, bf16[4,16,4,16,512]{4,3,2,1,0:T(8,128)(2,1)}, u32[]{:S(2)}) copy-start(bf16[4,16,4,16,512]{4,3,2,1,0:T(8,128)(2,1)} %param.6) | copy-start | bytes 12582916
  78.0 29.5 %all-to-all-start.3 = ((bf16[4,4,4,4,8,512]{5,4,3,2,1,0:T(8,128)(2,1)}), bf16[4,4,4,4,8,512]{5,4,3,2,1,0:T(8,128)(2,1)}, u32[]{:S(2)}, u32[]{:S(2)}) async-start(bf16[4,4,4,4,8,512]{5,4,3,2,1,0:T(8,128)(2,1)} %copy.70), calls=%async_computation.3 | async-start | bytes 4194304 | tf_op jit(solution)/shard_map/all_to_all | solution.py:31
  84.9 2.0 %copy-start.5 = (bf16[1,16,4,16,512]{4,3,2,1,0:T(8,128)(2,1)S(1)}, bf16[1,16,4,16,512]{4,3,2,1,0:T(8,128)(2,1)}, u32[]{:S(2)}) copy-start(bf16[1,16,4,16,512]{4,3,2,1,0:T(8,128)(2,1)} %get-tuple-element.10) | copy-start | bytes 3145732
  86.9 1.2 copy-start.4
  87.4 1.3 copy-start.3
  88.6 1.2 copy-start.2
  107.5 11.2 %all-to-all-start.1 = ((bf16[4,2,32768]{2,1,0:T(2,128)(2,1)}), bf16[4,2,32768]{2,1,0:T(2,128)(2,1)}, u32[]{:S(2)}, u32[]{:S(2)}) async-start(bf16[4,2,32768]{2,1,0:T(2,128)(2,1)} %reshape.54), calls=%async_computation.1 | async-start | bytes 1048576 | tf_op jit(solution)/shard_map/all_to_all | solution.py:71
where the time goes:
time: 183 us; the launch traced here: 182 us
  waiting for transfers between devices  51.2 us (28%)
  local copies, waits for them, and re-layouts  47 us (26%)
  blocking collectives  38.1 us (21%)
  starting transfers between devices  29.1 us (16%)
  matrix products  13.1 us (7%)
  other arithmetic  3.22 us (2%)
    all_to_all x1, blocking collectives, shards(): lax.all_to_all(synthesis, 'freq', split_axis=3, concat_axis=0, tiled=True)  38.1 us
    all_to_all x2, waiting for transfers between devices, cut_exchange(): lax.all_to_all(piece, axis, split_axis=0, concat_axis=0, tiled=True)  27.5 us
    all_to_all x1, waiting for transfers between devices, shards(): lax.all_to_all(spectra_local, 'freq', split_axis=0, concat_axis=3, tiled=...  22.2 us
    unnamed x20, local copies, waits for them, and re-layouts  21.5 us
    all_to_all x1, starting transfers between devices, shards(): lax.all_to_all(spectra_local, 'freq', split_axis=0, concat_axis=3, tiled=...  15.5 us
    all_to_all x2, starting transfers between devices, cut_exchange(): lax.all_to_all(piece, axis, split_axis=0, concat_axis=0, tiled=True)  9.29 us
    split x3, local copies, waits for them, and re-layouts, cut_exchange(): jnp.split(parts, cut_rows(parts.shape[cut], pieces), axis=cut)  8.9 us
    dot_general x1, matrix products, shards(): jnp.einsum('krws,tk->rswt', lax.all_to_all(synthesis, 'freq', split_axis=...  4.76 us
  transfers between devices with their start and end apart: 4, of which 4 were waited for; matrix products, arithmetic and copies ran while one was open for 17% of the time, Pallas kernels for 0%

commit v1 on v0

v1 whole, which is shorter than its diff:
```python
import jax
import jax.numpy as jnp
import numpy as np
from jax import lax
from jax.experimental import pallas as pl
from jax.experimental.pallas import tpu as pltpu
from jax.sharding import PartitionSpec as P

MESH = pl.DeviceIdType.MESH
F32, BF16 = jnp.float32, jnp.bfloat16
NZ, NY, NC, NX = 8, 4, 2, 4
NFREQ = NZ * NY * NC
KL = 4


def hartley_rows(time_count, freq_count):
    phase = np.arange(freq_count)[:, None] * np.arange(time_count)[None, :] % time_count
    angle = np.float32(2.0 * np.pi / time_count) * phase.astype(np.float32)
    table = (np.cos(angle) + np.sin(angle)) / np.sqrt(np.float32(time_count))
    return jnp.asarray(table.astype(np.float32)).astype(BF16)


def freq_peer(f, i):
    z, y, c = f // (NY * NC), lax.rem(f // NC, NY), lax.rem(f, NC)
    dz, dy, dc = lax.rem(i, NZ), lax.rem(i // NZ, NY), i // (NZ * NY)
    return (lax.rem(z + dz, NZ) * NY + lax.rem(y + dy, NY)) * NC + lax.rem(c + dc, NC)


def kernel(
    cas, ranks, traces, left, right, out,
    tr, rt, lall, stage, send, recv, csend, crecv, send2, recv2, stage2, outv,
    local_sem, spec_sem, left_sem, coef_sem, syn_sem, out_sem,
):
    f, x = lax.axis_index("freq"), lax.axis_index("col")

    def spec_copy(i, k):
        d = freq_peer(f, i)
        return pltpu.make_async_remote_copy(
            send.at[d, k], recv.at[f, k], spec_sem.at[0, k], spec_sem.at[1, k],
            device_id=(d, x), device_id_type=MESH,
        )

    def syn_copy(i, k):
        d = freq_peer(f, i)
        return pltpu.make_async_remote_copy(
            send2.at[d, k], recv2.at[f, k], syn_sem.at[0, k], syn_sem.at[1, k],
            device_id=(d, x), device_id_type=MESH,
        )

    def left_copy(o, k):
        d = lax.rem(x + o, NX)
        return pltpu.make_async_remote_copy(
            left.at[k, pl.ds(4 * d, 4)], lall.at[k, :, x], left_sem.at[0, k], left_sem.at[1, k],
            device_id=(f, d), device_id_type=MESH,
        )

    def coef_copy(o, k):
        d = lax.rem(x + o, NX)
        return pltpu.make_async_remote_copy(
            csend.at[k, d], crecv.at[k, x], coef_sem.at[0, k], coef_sem.at[1, k],
            device_id=(f, d), device_id_type=MESH,
        )

    def whole(src, dst, sems, k):
        return pltpu.make_async_remote_copy(
            src, dst, sems.at[0, k], sems.at[1, k], device_id=(f, x), device_id_type=MESH
        )

    rest = pl.ds(0, NFREQ - 1)

    def spec_all(k):
        return whole(send.at[rest, k], recv.at[rest, k], spec_sem, k)

    def syn_all(k):
        return whole(send2.at[rest, k], recv2.at[rest, k], syn_sem, k)

    def left_all(k):
        return whole(left.at[k, pl.ds(0, 12)], lall.at[k, :, pl.ds(0, 3)], left_sem, k)

    def coef_all(k):
        return whole(csend.at[k, pl.ds(0, 3)], crecv.at[k, pl.ds(0, 3)], coef_sem, k)

    barrier = pltpu.get_barrier_semaphore()

    def greet(i, carry):
        pl.semaphore_signal(
            barrier, inc=1, device_id=(freq_peer(f, i), x), device_id_type=MESH
        )
        return carry

    lax.fori_loop(1, NFREQ, greet, 0)
    for o in range(1, NX):
        pl.semaphore_signal(
            barrier, inc=1, device_id=(f, lax.rem(x + o, NX)), device_id_type=MESH
        )

    traces_in = pltpu.make_async_copy(traces, tr, local_sem.at[0])
    right_in = pltpu.make_async_copy(right, rt, local_sem.at[1])
    left_in = pltpu.make_async_copy(left.at[:, pl.ds(4 * x, 4)], lall.at[:, :, x], local_sem.at[2])
    traces_in.start()
    right_in.start()
    left_in.start()

    pl.semaphore_wait(barrier, NFREQ - 1 + NX - 1)
    for k in range(KL):
        for o in (1, 3, 2):
            left_copy(o, k).start()

    traces_in.wait()

    def spectra(n, carry):
        p, s = n // 8, lax.rem(n, 8)
        rows = jnp.concatenate([tr[2 * p, s], tr[2 * p + 1, s]], axis=0)
        acc = lax.dot_general(
            cas[...], rows, (((1,), (1,)), ((), ())), preferred_element_type=F32
        )
        stage[p, pl.ds(s, 256, 8), :] = acc
        return carry

    lax.fori_loop(0, 16, spectra, 0)

    def pack(n, carry):
        halves = [stage[p, pl.ds(n * 256, 256), :].reshape(8, KL, 8, 128) for p in range(2)]
        send[pl.ds(n * 8, 8)] = jnp.concatenate(halves, axis=2).astype(BF16)
        return carry

    lax.fori_loop(0, 8, pack, 0)

    def start_spec(n, carry):
        k, i = n // NFREQ, lax.rem(n, NFREQ)

        @pl.when(i > 0)
        def _():
            spec_copy(i, k).start()

        return carry

    lax.fori_loop(0, KL * NFREQ, start_spec, 0)
    recv[pl.ds(f, 1)] = send[pl.ds(f, 1)]
    right_in.wait()

    lane = lax.broadcasted_iota(jnp.int32, (256, 128), 1)
    rank_index = lax.rem(lax.broadcasted_iota(jnp.int32, (256, 128), 0), 16)

    def coeffs(k):
        spec_all(k).wait_recv()
        spectrum = recv[:, k].astype(F32)
        for p in range(2):
            rows = spectrum[:, 8 * p : 8 * p + 8].reshape(512, 128).astype(BF16)
            products = [
                jnp.dot(rt[k, :, 2 * p + b].reshape(256, 512), rows, preferred_element_type=F32)
                for b in range(2)
            ]
            limits = jnp.where(
                lax.broadcasted_iota(jnp.int32, (16, 128), 1) < 64,
                jnp.broadcast_to(ranks[k, :, 2 * p : 2 * p + 1], (16, 128)),
                jnp.broadcast_to(ranks[k, :, 2 * p + 1 : 2 * p + 2], (16, 128)),
            )
            limits = jnp.concatenate(
                [jnp.broadcast_to(limits[r : r + 1], (16, 128)) for r in range(16)], axis=0
            )
            kept = jnp.where(lane < 64, products[0], products[1])
            kept = jnp.where(rank_index < limits, kept, 0.0).astype(BF16)
            csend[k, :, p] = kept.reshape(4, 64, 128)
        crecv[k, pl.ds(x, 1)] = csend[k, pl.ds(x, 1)]
        for o in (1, 3, 2):
            coef_copy(o, k).start()

    def synthesis(k):
        coef_all(k).wait_recv()
        left_all(k).wait_recv()
        sums = []
        for r in range(4):
            mine = crecv[k, :, :, 16 * r : 16 * r + 16].reshape(128, 128)
            turned = mine.astype(F32).T.astype(BF16)
            lhs = jnp.concatenate([turned[:64], turned[64:]], axis=1)
            rhs = jnp.concatenate(
                [lall[k, r, :, :, b].reshape(128, 512) for b in range(2)], axis=0
            )
            sums.append(jnp.dot(lhs, rhs, preferred_element_type=F32))
        halves = [
            jnp.concatenate(sums[2 * q : 2 * q + 2], axis=0).T.reshape(64, 8, 128) for q in range(2)
        ]
        send2[:, k] = jnp.concatenate(halves, axis=1).astype(BF16)
        recv2[pl.ds(f, 1), k] = send2[pl.ds(f, 1), k]

        def start(i, carry):
            syn_copy(i, k).start()
            return carry

        lax.fori_loop(1, NFREQ, start, 0)

    coeffs(0)
    left_in.wait()

    def both(k, carry):
        coeffs(k + 1)
        synthesis(k)
        return carry

    lax.fori_loop(0, KL - 1, both, 0)
    synthesis(KL - 1)

    def gather(k, carry):
        syn_all(k).wait_recv()

        def one(n, inner):
            stage2[pl.ds(n * 64 + k * 16, 16), :] = recv2[n, k].astype(F32)
            return inner

        lax.fori_loop(0, NFREQ, one, 0, unroll=8)
        return carry

    lax.fori_loop(0, KL, gather, 0)

    def inverse(n, carry):
        q, s = n // 8, lax.rem(n, 8)
        rows = stage2[pl.ds(n, 256, 16), :].T.astype(BF16)
        acc = jnp.dot(rows, cas[...], preferred_element_type=F32).astype(BF16)
        outv[2 * q, s] = acc[:64]
        outv[2 * q + 1, s] = acc[64:]
        return carry

    out_copies = [
        pltpu.make_async_copy(outv.at[pl.ds(2 * q, 2)], out.at[pl.ds(2 * q, 2)], out_sem.at[q])
        for q in range(2)
    ]
    for q in range(2):
        lax.fori_loop(8 * q, 8 * q + 8, inverse, 0)
        out_copies[q].start()
    for k in range(KL):
        spec_all(k).wait_send()
        left_all(k).wait_send()
        coef_all(k).wait_send()
        syn_all(k).wait_send()
    for q in range(2):
        out_copies[q].wait()


def shards(traces, left_factors, right_factors, tile_ranks):
    cas = hartley_rows(512, 256)
    vmem = pl.BlockSpec(memory_space=pltpu.VMEM)
    hbm = pl.BlockSpec(memory_space=pl.ANY)
    return pl.pallas_call(
        kernel,
        out_shape=jax.ShapeDtypeStruct((4, 8, 64, 512), BF16),
        in_specs=[vmem, vmem, hbm, hbm, hbm],
        out_specs=hbm,
        scratch_shapes=[
            pltpu.VMEM((4, 8, 64, 512), BF16),
            pltpu.VMEM((4, 16, 4, 16, 512), BF16),
            pltpu.VMEM((4, 4, 4, 2, 2, 16, 512), BF16),
            pltpu.VMEM((2, 2048, 128), F32),
            pltpu.VMEM((64, 4, 16, 128), BF16),
            pltpu.VMEM((64, 4, 16, 128), BF16),
            pltpu.VMEM((4, 4, 2, 64, 128), BF16),
            pltpu.VMEM((4, 4, 2, 64, 128), BF16),
            pltpu.VMEM((64, 4, 16, 128), BF16),
            pltpu.VMEM((64, 4, 16, 128), BF16),
            pltpu.VMEM((4096, 128), F32),
            pltpu.VMEM((4, 8, 64, 512), BF16),
            pltpu.SemaphoreType.DMA((3,)),
            pltpu.SemaphoreType.DMA((2, KL)),
            pltpu.SemaphoreType.DMA((2, KL)),
            pltpu.SemaphoreType.DMA((2, KL)),
            pltpu.SemaphoreType.DMA((2, KL)),
            pltpu.SemaphoreType.DMA((2,)),
        ],
        compiler_params=pltpu.CompilerParams(
            collective_id=0, has_side_effects=True, vmem_limit_bytes=48 << 20
        ),
        cost_estimate=pl.CostEstimate(flops=2 * 10**9, bytes_accessed=16 << 20, transcendentals=0),
        name="tiles",
    )(
        cas,
        tile_ranks,
        traces,
        left_factors.reshape(4, 16, 2, 2, 16, 512),
        right_factors,
    )


def solution(mesh):
    in_specs = (
        P("col", "freq", None, None),
        P("freq", None, "col", None, None),
        P("freq", None, "col", None, None),
        P("freq", None, "col"),
    )
    out_specs = P("col", "freq", None, None)
    return jax.shard_map(shards, mesh=mesh, in_specs=in_specs, out_specs=out_specs, check_vma=False)
```

time: 183 us -> 98.8 us (0.54)
  Pallas kernels: 0 us -> 94 us
  waiting for transfers between devices: 51.2 us -> 0 us
  local copies, waits for them, and re-layouts: 47 us -> 4.65 us
  blocking collectives: 38.1 us -> 0 us
  starting transfers between devices: 29.1 us -> 0 us
  matrix products: 13.1 us -> 0 us
  other arithmetic: 3.22 us -> 0 us
    pallas_call x0 -> x1, Pallas kernels: none -> 94 us  [shards(): pl.pallas_call(kernel, out_shape=jax.ShapeDtypeStruct((4, 8, 64, 512), BF...]
    all_to_all x4 -> x0, waiting for transfers between devices: 51.2 us -> none  [the longest x2 27.5 us: cut_exchange(): lax.all_to_all(piece, axis, split_axis=0, concat_axis=0, tiled=True)]
    all_to_all x1 -> x0, blocking collectives: 38.1 us -> none  [shards(): lax.all_to_all(synthesis, 'freq', split_axis=3, concat_axis=0, tiled=True)]
    all_to_all x4 -> x0, starting transfers between devices: 29.1 us -> none  [the longest x1 15.5 us: shards(): lax.all_to_all(spectra_local, 'freq', split_axis=0, concat_axis=3, tiled=...]
    unnamed x20 -> x6, local copies, waits for them, and re-layouts: 21.5 us -> 4.65 us
    dot_general x7 -> x0, matrix products: 13.1 us -> none  [the longest x1 4.76 us: shards(): jnp.einsum('krws,tk->rswt', lax.all_to_all(synthesis, 'freq', split_axis=...]
    split x3 -> x0, local copies, waits for them, and re-layouts: 8.9 us -> none  [cut_exchange(): jnp.split(parts, cut_rows(parts.shape[cut], pieces), axis=cut)]
    convert_element_type x2 -> x0, local copies, waits for them, and re-layouts: 6.73 us -> none  [the longest x1 3.81 us: shards(): spectra_local = jnp.einsum('cswt,tk->kcws', traces, cas_table, preferred_...]
  transfers between devices with their start and end apart: 4 -> 0, of which waited for: 4 -> 0; matrix products, arithmetic and copies ran while one was open for 17% -> 0% of each run, Pallas kernels for 0% -> 0%
where the time goes in v1:
time: 98.8 us; the launch traced here: 98.6 us
  Pallas kernels  94 us (95%)
  local copies, waits for them, and re-layouts  4.65 us (5%)
    pallas_call x1, Pallas kernels, shards(): pl.pallas_call(kernel, out_shape=jax.ShapeDtypeStruct((4, 8, 64, 512), BF...  94 us
    unnamed x6, local copies, waits for them, and re-layouts  4.65 us

profile of v1, /device:TPU:1, one launch (start us, length us, event | category | flops | bytes accessed | tf_op | source)
XLA Modules:
  0.0 98.6 jit_solution(2123538649504011500)
XLA Ops:
  0.0 0.8 copy.6.ranks
  0.8 0.0 copy-start
  0.8 1.6 %copy-done = bf16[4,8,64,512]{3,2,1,0:T(8,128)(2,1)S(1)} copy-done((bf16[4,8,64,512]{3,2,1,0:T(8,128)(2,1)S(1)}, bf16[4,8,64,512]{3,2,1,0:T(8,128)(2,1)}, u32[]{:S(2)}) %copy-start) | copy-done | bytes 2097176
  2.4 0.0 copy-start.1
  2.4 0.9 copy-done.1
  3.3 94.0 %tiles.1 = bf16[4,8,64,512]{3,2,1,0:T(8,128)(2,1)S(1)} custom-call(bf16[256,512]{1,0:T(8,128)(2,1)S(1)} %copy-done.1, s32[4,16,4]{2,1,0:T(8,128)S(1)} %copy.6.ranks, bf16[4,8,64,512]{3,2,1,0:T(8,128)(2,1)S(1)} %copy-done, bf16[4,16,2,2,16,512]{5,4,3,2,1,0:T(8,128)(2,1)} %bitcast.1, bf16[4,16,4,16,512]{4,3,2,1,0:T(8,128)(2,1)} %right.1), custom_call_target="tpu_custom_call" | custom-call | flops 2000000000 | bytes 16777216 | tf_op jit(solution)/shard_map/tiles/pallas_call | solution.py:244
  97.3 1.3 %copy.8 = bf16[4,8,64,512]{3,2,1,0:T(8,128)(2,1)} copy(bf16[4,8,64,512]{3,2,1,0:T(8,128)(2,1)S(1)} %tiles.1) | data formatting | bytes 4194304
Async XLA Ops:
  0.8 1.6 %copy-start = (bf16[4,8,64,512]{3,2,1,0:T(8,128)(2,1)S(1)}, bf16[4,8,64,512]{3,2,1,0:T(8,128)(2,1)}, u32[]{:S(2)}) copy-start(bf16[4,8,64,512]{3,2,1,0:T(8,128)(2,1)} %traces.1) | copy-start | bytes 6291460
  2.4 0.9 copy-start.1

commit v2 on v1

v2 whole, which is shorter than its diff:
```python
import jax
import jax.numpy as jnp
import numpy as np
from jax import lax
from jax.experimental import pallas as pl
from jax.experimental.pallas import tpu as pltpu
from jax.sharding import PartitionSpec as P

MESH = pl.DeviceIdType.MESH
F32, BF16 = jnp.float32, jnp.bfloat16
NZ, NY, NC, NX = 8, 4, 2, 4
NFREQ = NZ * NY * NC
KL = 4
PART = 8


def hartley_rows(time_count, freq_count, stride=1):
    freqs = np.arange(freq_count).reshape(-1, stride).T.reshape(-1)
    phase = freqs[:, None] * np.arange(time_count)[None, :] % time_count
    angle = np.float32(2.0 * np.pi / time_count) * phase.astype(np.float32)
    table = (np.cos(angle) + np.sin(angle)) / np.sqrt(np.float32(time_count))
    return jnp.asarray(table.astype(np.float32)).astype(BF16)


def freq_peer(f, i):
    z, y, c = f // (NY * NC), lax.rem(f // NC, NY), lax.rem(f, NC)
    dz, dy, dc = lax.rem(i, NZ), lax.rem(i // NZ, NY), i // (NZ * NY)
    return (lax.rem(z + dz, NZ) * NY + lax.rem(y + dy, NY)) * NC + lax.rem(c + dc, NC)


def kernel(
    cas_in, ranks, traces, left, right, out,
    cas, limits, tr, rt, lloc, lrecv, hold, chain, stage, send, recv, csend, crecv, send2, recv2, stage2, turned_rows,
    local_sem, spec_sem, left_sem, coef_sem, chain_sem, syn_sem, out_sem,
):
    f, x = lax.axis_index("freq"), lax.axis_index("col")
    after, before, across = lax.rem(x + 1, NX), lax.rem(x + NX - 1, NX), lax.rem(x + 2, NX)
    routes = [(across, 0, after), (after, 1, after), (across, 1, before), (before, 0, before)]

    def spec_copy(i, k):
        d = freq_peer(f, i)
        return pltpu.make_async_remote_copy(
            send.at[d, k], recv.at[f, k], spec_sem.at[0, k], spec_sem.at[1, k],
            device_id=(d, x), device_id_type=MESH,
        )

    def syn_copy(i, k):
        d = freq_peer(f, i)
        return pltpu.make_async_remote_copy(
            send2.at[d, k], recv2.at[f, k], syn_sem.at[0, k], syn_sem.at[1, k],
            device_id=(d, x), device_id_type=MESH,
        )

    def left_copy(slot, k):
        owner, q, d = routes[slot]
        return pltpu.make_async_remote_copy(
            left.at[k, pl.ds(4 * owner + 2 * q, 2)], lrecv.at[k, slot],
            left_sem.at[0, k, slot], left_sem.at[1, k, slot],
            device_id=(f, d), device_id_type=MESH,
        )

    def coef_copy(slot, k):
        owner, q, d = routes[slot]
        return pltpu.make_async_remote_copy(
            csend.at[k, owner, q], crecv.at[k, slot],
            coef_sem.at[0, k, slot], coef_sem.at[1, k, slot],
            device_id=(f, d), device_id_type=MESH,
        )

    def chain_copy(q, k):
        return pltpu.make_async_remote_copy(
            chain.at[0, k, q], chain.at[1, k, q], chain_sem.at[0, k, q], chain_sem.at[1, k, q],
            device_id=(f, (after, before)[q]), device_id_type=MESH,
        )

    def whole(src, dst, sems, k):
        return pltpu.make_async_remote_copy(
            src, dst, sems.at[0, k], sems.at[1, k], device_id=(f, x), device_id_type=MESH
        )

    rest = pl.ds(0, NFREQ - 1)

    def spec_all(k):
        return whole(send.at[rest, k], recv.at[rest, k], spec_sem, k)

    def syn_all(k):
        return whole(send2.at[rest, k], recv2.at[rest, k], syn_sem, k)

    def far_left(k):
        left_copy(0, k).start()
        left_copy(2, k).start()

    def near_left(k):
        left_copy(1, k).start()
        left_copy(3, k).start()

    traces_in = pltpu.make_async_copy(traces, tr, local_sem.at[0])
    right_in = pltpu.make_async_copy(right, rt, local_sem.at[1])
    left_in = pltpu.make_async_copy(left, lloc, local_sem.at[2])
    cas_load = pltpu.make_async_copy(cas_in, cas, local_sem.at[3])
    traces_in.start()
    cas_load.start()
    right_in.start()
    left_in.start()

    barrier = pltpu.get_barrier_semaphore()

    def greet(i, carry):
        pl.semaphore_signal(
            barrier, inc=1, device_id=(freq_peer(f, i), x), device_id_type=MESH
        )
        return carry

    lax.fori_loop(1, NFREQ, greet, 0)
    for d in (after, before):
        pl.semaphore_signal(barrier, inc=1, device_id=(f, d), device_id_type=MESH)

    cas_load.wait()
    traces_in.wait()

    def spectra(n, carry):
        p, s = n // 4, 2 * lax.rem(n, 4)
        rows = jnp.concatenate(
            [tr[2 * p, s], tr[2 * p + 1, s], tr[2 * p, s + 1], tr[2 * p + 1, s + 1]], axis=0
        )
        acc = lax.dot_general(
            cas[...], rows, (((1,), (1,)), ((), ())), preferred_element_type=F32
        )
        stage[p, pl.ds(s, 256, 8), :] = acc[:, :128]
        stage[p, pl.ds(s + 1, 256, 8), :] = acc[:, 128:]
        return carry

    lax.fori_loop(0, 8, spectra, 0, unroll=2)

    def pack(n, carry):
        halves = [stage[p, pl.ds(n * 256, 256), :].reshape(8, KL, 8, 128) for p in range(2)]
        send[pl.ds(n * 8, 8)] = jnp.concatenate(halves, axis=2).astype(BF16)
        return carry

    lax.fori_loop(0, 8, pack, 0)

    row16 = lax.broadcasted_iota(jnp.int32, (16, 16), 0)
    diagonal = row16 == lax.broadcasted_iota(jnp.int32, (16, 16), 1)
    low_half = lax.broadcasted_iota(jnp.int32, (16, 128), 1) < 64
    for k in range(KL):
        for p in range(2):
            columns = [
                jnp.sum(
                    jnp.where(diagonal, ranks[k, 2 * p + b : 2 * p + b + 1].astype(F32), 0.0),
                    axis=1, keepdims=True,
                )
                for b in range(2)
            ]
            limits[k, p] = jnp.where(
                low_half, jnp.broadcast_to(columns[0], (16, 128)), jnp.broadcast_to(columns[1], (16, 128))
            )

    pl.semaphore_wait(barrier, NFREQ - 1 + 2)
    far_left(0)
    near_left(0)
    far_left(1)
    near_left(1)

    def start_spec(n, carry):
        k, i = n // NFREQ, lax.rem(n, NFREQ)

        @pl.when(i > 0)
        def _():
            spec_copy(i, k).start()

        return carry

    lax.fori_loop(0, KL * NFREQ, start_spec, 0)
    recv[pl.ds(f, 1)] = send[pl.ds(f, 1)]
    right_in.wait()

    lane = lax.broadcasted_iota(jnp.int32, (256, 128), 1)
    rank_index = lax.rem(lax.broadcasted_iota(jnp.int32, (256, 128), 0), 16).astype(F32)

    def coeffs(k):
        spec_all(k).wait_recv()
        spectrum = recv[:, k].astype(F32)
        for p in range(2):
            rows = spectrum[:, 8 * p : 8 * p + 8].reshape(512, 128).astype(BF16)
            products = [
                jnp.dot(rt[k, :, 2 * p + b].reshape(256, 512), rows, preferred_element_type=F32)
                for b in range(2)
            ]
            bound = jnp.concatenate(
                [jnp.broadcast_to(limits[k, p, r : r + 1], (16, 128)) for r in range(16)], axis=0
            )
            kept = jnp.where(lane < 64, products[0], products[1])
            kept = jnp.where(rank_index < bound, kept, 0.0).astype(BF16)
            csend[k, :, :, p] = kept.reshape(4, 2, 32, 128)
        for slot in (0, 2, 1, 3):
            coef_copy(slot, k).start()

    def spread(k, pairs):
        halves = [pair.T.reshape(64, 8, 128) for pair in pairs]
        send2[:, k] = jnp.concatenate(halves, axis=1).astype(BF16)
        recv2[pl.ds(f, 1), k] = send2[pl.ds(f, 1), k]

        def start(i, carry):
            syn_copy(i, k).start()
            return carry

        lax.fori_loop(1, NFREQ, start, 0)

    half = lax.broadcasted_iota(jnp.int32, (64, 256), 1) // 16 % 2

    def pair_sum(k, owner, q, slot):
        coefs = jnp.concatenate(
            [csend[k, owner, q].reshape(64, 128), crecv[k, slot].reshape(64, 128)], axis=0
        )
        turned = coefs.astype(F32).T
        lanes = jnp.concatenate([turned[:64], turned[64:]], axis=1)
        lhs = jnp.concatenate([jnp.where(half == r, lanes, 0.0) for r in range(2)], axis=0)
        rhs = []
        for b in range(2):
            rhs += [lloc[k, pl.ds(4 * owner + 2 * q, 2), p, b].reshape(32, 512) for p in range(2)]
            rhs += [lrecv[k, slot, :, p, b].reshape(32, 512) for p in range(2)]
        return jnp.dot(
            lhs.astype(BF16), jnp.concatenate(rhs, axis=0), preferred_element_type=F32
        )

    def arrived(k, slot):
        left_copy(slot, k).wait_recv()
        coef_copy(slot, k).wait_recv()

    def sums(k):
        arrived(k, 0)
        chain[0, k, 0] = pair_sum(k, after, 0, 0).astype(BF16)
        chain_copy(0, k).start()
        arrived(k, 2)
        chain[0, k, 1] = pair_sum(k, before, 1, 2).astype(BF16)
        chain_copy(1, k).start()

    def own_sums(k):
        arrived(k, 3)
        hold[k, 0] = pair_sum(k, x, 0, 3)
        arrived(k, 1)
        hold[k, 1] = pair_sum(k, x, 1, 1)

    def finish(k):
        for q in range(2):
            chain_copy(q, k).wait_recv()
        spread(k, [hold[k, q] + chain[1, k, q].astype(F32) for q in range(2)])

    steps = ["C0", "A2", "C1", "W", "X0", "B2", "Y0", "C2", "F0", "A3", "X1", "B3", "Y1", "C3", "F1", "X2", "X3", "Y2", "F2", "Y3", "F3"]
    for step in steps:
        if step == "W":
            left_in.wait()
            continue
        dict(C=coeffs, A=far_left, B=near_left, X=sums, Y=own_sums, F=finish)[step[0]](int(step[1]))

    def lanes_out(h):
        part = (slice(None), pl.ds(128 * h, 128))
        return pltpu.make_async_copy(turned_rows.at[part], out.at[part], out_sem.at[h])

    for k in range(KL):
        syn_all(k).wait_recv()
        stage2[...] = recv2[:, k].astype(F32).reshape(1024, 128)
        for n in range(16):
            turned_rows[128 * n : 128 * n + 128, 64 * k : 64 * k + 64] = (
                stage2[pl.ds(n, 64, 16), :].astype(BF16).T
            )

        if k % 2:
            lanes_out(k // 2).start()
    for k in range(KL):
        spec_all(k).wait_send()
        syn_all(k).wait_send()
        for slot in range(4):
            left_copy(slot, k).wait_send()
            coef_copy(slot, k).wait_send()
        for q in range(2):
            chain_copy(q, k).wait_send()
    for h in range(2):
        lanes_out(h).wait()


def inverse(rows, cas, out):
    acc = jnp.dot(rows[...], cas[...], preferred_element_type=F32).astype(BF16)
    for b in range(acc.shape[0] // 128):
        out[0, b] = acc[128 * b : 128 * b + 64]
        out[1, b] = acc[128 * b + 64 : 128 * b + 128]


def shards(traces, left_factors, right_factors, tile_ranks):
    cas = hartley_rows(512, 256)
    vmem = pl.BlockSpec(memory_space=pltpu.VMEM)
    hbm = pl.BlockSpec(memory_space=pl.ANY)
    turned_rows = pl.pallas_call(
        kernel,
        out_shape=jax.ShapeDtypeStruct((2048, 256), BF16),
        in_specs=[hbm, vmem, hbm, hbm, hbm],
        out_specs=hbm,
        scratch_shapes=[
            pltpu.VMEM((256, 512), BF16),
            pltpu.VMEM((4, 2, 16, 128), F32),
            pltpu.VMEM((4, 8, 64, 512), BF16),
            pltpu.VMEM((4, 16, 4, 16, 512), BF16),
            pltpu.VMEM((4, 16, 2, 2, 16, 512), BF16),
            pltpu.VMEM((4, 4, 2, 2, 2, 16, 512), BF16),
            pltpu.VMEM((4, 2, 128, 512), F32),
            pltpu.VMEM((2, 4, 2, 128, 512), BF16),
            pltpu.VMEM((2, 2048, 128), F32),
            pltpu.VMEM((64, 4, 16, 128), BF16),
            pltpu.VMEM((64, 4, 16, 128), BF16),
            pltpu.VMEM((4, 4, 2, 2, 32, 128), BF16),
            pltpu.VMEM((4, 4, 2, 32, 128), BF16),
            pltpu.VMEM((64, 4, 16, 128), BF16),
            pltpu.VMEM((64, 4, 16, 128), BF16),
            pltpu.VMEM((1024, 128), F32),
            pltpu.VMEM((2048, 256), BF16),
            pltpu.SemaphoreType.DMA((4,)),
            pltpu.SemaphoreType.DMA((2, KL)),
            pltpu.SemaphoreType.DMA((2, KL, 4)),
            pltpu.SemaphoreType.DMA((2, KL, 4)),
            pltpu.SemaphoreType.DMA((2, KL, 2)),
            pltpu.SemaphoreType.DMA((2, KL)),
            pltpu.SemaphoreType.DMA((2,)),
        ],
        compiler_params=pltpu.CompilerParams(
            collective_id=0, has_side_effects=True, vmem_limit_bytes=60 << 20
        ),
        cost_estimate=pl.CostEstimate(flops=2 * 10**9, bytes_accessed=16 << 20, transcendentals=0),
        name="tiles",
    )(
        cas,
        jnp.transpose(tile_ranks, (0, 2, 1)),
        traces,
        left_factors.reshape(4, 16, 2, 2, 16, 512),
        right_factors,
    )
    return pl.pallas_call(
        inverse,
        grid=(2, 8 // PART),
        out_shape=jax.ShapeDtypeStruct((4, 8, 64, 512), BF16),
        in_specs=[
            pl.BlockSpec((128 * PART, 256), lambda q, n: (q * (8 // PART) + n, 0)),
            pl.BlockSpec((256, 512), lambda q, n: (0, 0)),
        ],
        out_specs=pl.BlockSpec((2, PART, 64, 512), lambda q, n: (q, n, 0, 0)),
        cost_estimate=pl.CostEstimate(flops=2**29, bytes_accessed=3 << 20, transcendentals=0),
        name="inverse",
    )(turned_rows, hartley_rows(512, 256, KL))


def solution(mesh):
    in_specs = (
        P("col", "freq", None, None),
        P("freq", None, "col", None, None),
        P("freq", None, "col", None, None),
        P("freq", None, "col"),
    )
    out_specs = P("col", "freq", None, None)
    return jax.shard_map(shards, mesh=mesh, in_specs=in_specs, out_specs=out_specs, check_vma=False)
```

time: 98.8 us -> 72.6 us (0.73)
  Pallas kernels: 94 us -> 72.4 us
  local copies, waits for them, and re-layouts: 4.65 us -> 0 us
    pallas_call x1 -> x2, Pallas kernels: 94 us -> 72.4 us  [the longest x1 69.5 us: shards(): pl.pallas_call(kernel, out_shape=jax.ShapeDtypeStruct((2048, 256), BF16),...]
    unnamed x6 -> x0, local copies, waits for them, and re-layouts: 4.65 us -> none
where the time goes in v2:
time: 72.6 us; the launch traced here: 72.5 us
  Pallas kernels  72.4 us (100%)
    pallas_call x1, Pallas kernels, shards(): pl.pallas_call(kernel, out_shape=jax.ShapeDtypeStruct((2048, 256), BF16),...  69.5 us
    pallas_call x1, Pallas kernels, shards(): pl.pallas_call(inverse, grid=(2, 8 // PART), out_shape=jax.ShapeDtypeStru...  2.98 us

profile of v2, /device:TPU:1, one launch (start us, length us, event | category | flops | bytes accessed | tf_op | source)
XLA Modules:
  0.0 72.5 jit_solution(7044757856917678407)
XLA Ops:
  0.0 69.5 %tiles.1.rows = bf16[2048,256]{1,0:T(8,128)(2,1)} custom-call(bf16[256,512]{1,0:T(8,128)(2,1)} %constant.10.cas_in, s32[4,4,16]{2,1,0:T(4,128)} %bitcast.3, bf16[4,8,64,512]{3,2,1,0:T(8,128)(2,1)} %traces.1, bf16[4,16,2,2,16,512]{5,4,3,2,1,0:T(8,128)(2,1)} %bitcast.2, bf16[4,16,4,16,512]{4,3,2,1,0:T(8,128)(2,1)} %right.1), custom_call_target="tpu_custom_call" | custom-call | flops 2000000000 | bytes 16777216 | tf_op jit(solution)/shard_map/tiles/pallas_call | solution.py:293
  69.5 3.0 %inverse.1 = bf16[4,8,64,512]{3,2,1,0:T(8,128)(2,1)} custom-call(bf16[2048,256]{1,0:T(8,128)(2,1)} %tiles.1.rows, bf16[256,512]{1,0:T(8,128)(2,1)} %constant.11.cas), custom_call_target="tpu_custom_call" | custom-call | flops 536870912 | bytes 3145728 | tf_op jit(solution)/shard_map/inverse/pallas_call | solution.py:336

commit v3 on v2

--- a/solution.py
+++ b/solution.py
@@ -246,7 +246,7 @@
             chain_copy(q, k).wait_recv()
         spread(k, [hold[k, q] + chain[1, k, q].astype(F32) for q in range(2)])
 
-    steps = ["C0", "A2", "C1", "W", "X0", "B2", "Y0", "C2", "F0", "A3", "X1", "B3", "Y1", "C3", "F1", "X2", "X3", "Y2", "F2", "Y3", "F3"]
+    steps = ["C0", "A2", "C1", "W", "X0", "B2", "Y0", "A3", "C2", "F0", "X1", "B3", "Y1", "C3", "F1", "X2", "X3", "Y2", "F2", "Y3", "F3"]
     for step in steps:
         if step == "W":
             left_in.wait()

time: 72.6 us -> 71.9 us (level)
  no operation moved by 1% of the time
where the time goes in v3:
time: 71.9 us; the launch traced here: 71.8 us
  Pallas kernels  71.8 us (100%)
    pallas_call x1, Pallas kernels, shards(): pl.pallas_call(kernel, out_shape=jax.ShapeDtypeStruct((2048, 256), BF16),...  68.8 us
    pallas_call x1, Pallas kernels, shards(): pl.pallas_call(inverse, grid=(2, 8 // PART), out_shape=jax.ShapeDtypeStru...  2.98 us

profile of v3, /device:TPU:1, one launch (start us, length us, event | category | flops | bytes accessed | tf_op | source)
XLA Modules:
  0.0 71.8 jit_solution(7894021303428379267)
XLA Ops:
  0.0 68.8 %tiles.1.rows = bf16[2048,256]{1,0:T(8,128)(2,1)} custom-call(bf16[256,512]{1,0:T(8,128)(2,1)} %constant.10.cas_in, s32[4,4,16]{2,1,0:T(4,128)} %bitcast.3, bf16[4,8,64,512]{3,2,1,0:T(8,128)(2,1)} %traces.1, bf16[4,16,2,2,16,512]{5,4,3,2,1,0:T(8,128)(2,1)} %bitcast.2, bf16[4,16,4,16,512]{4,3,2,1,0:T(8,128)(2,1)} %right.1), custom_call_target="tpu_custom_call" | custom-call | flops 2000000000 | bytes 16777216 | tf_op jit(solution)/shard_map/tiles/pallas_call | solution.py:293
  68.8 3.0 %inverse.1 = bf16[4,8,64,512]{3,2,1,0:T(8,128)(2,1)} custom-call(bf16[2048,256]{1,0:T(8,128)(2,1)} %tiles.1.rows, bf16[256,512]{1,0:T(8,128)(2,1)} %constant.11.cas), custom_call_target="tpu_custom_call" | custom-call | flops 536870912 | bytes 3145728 | tf_op jit(solution)/shard_map/inverse/pallas_call | solution.py:336
